TPU v7x, 512 devices: a whole 4x8x8 slice. The times are simulated.
512 devices in a mesh: pair: 128 (over x_hi, y, z), row: 4 (over x_lo, core).
Axes of the slice: x: 4 (x_hi: 2, x_lo: 2; x = x_hi * 2 + x_lo), y: 8, z: 8, core: 2. Of those that a mesh axis runs over, the one named last changes fastest.
Arguments:
- statistic: bfloat16 [16384, 16384], P('row', 'pair'), may hold values from -1 to 12, as said below
- initial_basis: bfloat16 [16384, 16384], P('row', 'pair'), may hold values from -6 to 6
- moving_slot: int32 [4, 128], P(None, 'pair'), may hold values from 0 to 1
Outputs:
- eigvectors: float32 [16384, 16384], P('row', 'pair')
- spectrum: float32 [16384], P('pair')
- off_ratio: float32 [4], replicated
Inputs may be any that keep to these rules, and one draw needn't show every extreme that they name: `statistic`: symmetric and positive definite. `moving_slot`: which of a pair's two blocks moves on.
All inputs are finite; a program needn't handle non-finite values.
Results may differ from a plain program's by a relative error of at most 0.0003.
Values sent between devices are 32-bit elements; how exact they have to be, the bound alone decides.
No kernel may reach another device: no remote copies, remote signals or barrier semaphores. Data moves between devices by JAX's collectives and lax.ppermute only.
A program may use at most 64 MiB of HBM per device.

v0:
```python
import jax
import jax.numpy as jnp
from jax import lax
from jax.sharding import PartitionSpec as P

ROUNDS = 4
HIGH = lax.Precision.HIGHEST


def from_behind(value, axis, steps):
    count = lax.axis_size(axis)
    pairs = [(source, (source + steps) % count) for source in range(count)]
    return lax.ppermute(value, axis, pairs)


def product(left, right):
    return jnp.dot(left, right, precision=HIGH, preferred_element_type=jnp.float32)


def inner_product(left, right):
    return lax.dot_general(
        left, right, (((0,), (0,)), ((), ())), precision=HIGH, preferred_element_type=jnp.float32
    )


def orthonormal(block):
    square = inner_product(block, block)
    lower = jnp.linalg.cholesky(square)
    return jax.scipy.linalg.solve_triangular(lower, block.T, lower=True).T


def rotation(gram):
    basis = orthonormal(gram)
    basis = orthonormal(product(gram, basis))
    return basis


def full_gram(factor):
    return lax.psum(inner_product(factor, factor), "row")


def on_device(statistic, initial_basis, moving_slot):
    rows, width = statistic.shape
    half = width // 2
    vectors = initial_basis.astype(jnp.float32)
    factor = statistic.astype(jnp.float32)
    mask = jnp.eye(width, dtype=bool)
    gram = full_gram(factor)
    ratios = []
    for step in range(ROUNDS):
        squares = gram * gram
        off_part = jnp.sum(jnp.where(mask, jnp.float32(0.0), squares))
        diag_part = jnp.sum(jnp.where(mask, squares, jnp.float32(0.0)))
        off_total, diag_total = lax.psum((off_part, diag_part), "pair")
        ratios.append(jnp.sqrt(off_total / diag_total))
        basis = rotation(gram)
        factor = product(factor, basis)
        vectors = product(vectors, basis)
        first_leaves = moving_slot[step, 0] == 0
        leaving = jnp.where(
            first_leaves,
            jnp.concatenate([factor[:, :half], vectors[:, :half]], axis=1),
            jnp.concatenate([factor[:, half:], vectors[:, half:]], axis=1),
        )
        stay_factor = jnp.where(first_leaves, factor[:, half:], factor[:, :half])
        stay_vectors = jnp.where(first_leaves, vectors[:, half:], vectors[:, :half])
        arrived = from_behind(leaving, "pair", 1)
        come_factor = arrived[:, :half]
        come_vectors = arrived[:, half:]
        factor = jnp.where(
            first_leaves,
            jnp.concatenate([come_factor, stay_factor], axis=1),
            jnp.concatenate([stay_factor, come_factor], axis=1),
        )
        vectors = jnp.where(
            first_leaves,
            jnp.concatenate([come_vectors, stay_vectors], axis=1),
            jnp.concatenate([stay_vectors, come_vectors], axis=1),
        )
        if step + 1 < ROUNDS:
            gram = full_gram(factor)
    off_ratio = jnp.stack(ratios)
    column_sq = lax.psum(jnp.sum(factor * factor, axis=0), "row")
    spectrum = jnp.sqrt(column_sq)
    return (vectors, spectrum, off_ratio)


def solution(mesh):
    return jax.shard_map(
        on_device,
        mesh=mesh,
        in_specs=(P("row", "pair"), P("row", "pair"), P(None, "pair")),
        out_specs=(P("row", "pair"), P("pair"), P()),
        check_vma=False,
    )
```

profile of v0, /device:TPU:1, one launch (start us, length us, event | category | flops | bytes accessed | tf_op | source)
XLA Modules:
  0.0 1018.9 jit_solution(724183624023404392)
XLA Ops:
  7.2 1.2 copy-done
  8.4 1.1 fusion.111
  10.9 52.7 %all-reduce.6.cloned.1.call-done = f32[128,128]{1,0:T(8,128)} async-done(((f32[128,128]{1,0:T(8,128)}), f32[128,128]{1,0:T(8,128)}) %all-reduce.6.cloned.1.call-update) | async-done | bytes 65552 | tf_op jit(solution)/shard_map/psum | solution.py:39
  63.6 1.2 fusion.112
  64.9 11.7 %cholesky.134 = f32[128,128]{1,0:T(8,128)S(1)} custom-call(f32[128,128]{1,0:T(8,128)S(1)} %fusion.74), custom_call_target="Cholesky" | custom-call | tf_op jit(solution)/shard_map/jit(cholesky)/cholesky | solution.py:28
  77.3 0.7 fusion.35
  78.0 9.8 custom-call.12
  87.8 1.1 fusion.71
  88.9 1.1 fusion.113
  90.4 11.7 %cholesky.145 = f32[128,128]{1,0:T(8,128)S(1)} custom-call(f32[128,128]{1,0:T(8,128)S(1)} %fusion.70), custom_call_target="Cholesky" | custom-call | tf_op jit(solution)/shard_map/jit(cholesky)/cholesky | solution.py:28
  102.8 0.7 fusion.36
  103.5 10.1 custom-call.13
  113.9 1.0 convolution_bitcast_fusion.1
  114.9 1.0 convolution_bitcast_fusion
  116.8 3.2 collective-permute-start
  120.0 52.6 %collective-permute-done = f32[4096,128]{0,1:T(8,128)S(1)} collective-permute-done((f32[4096,128]{0,1:T(8,128)S(1)}, f32[4096,128]{0,1:T(8,128)S(1)}, u32[]{:S(2)}, u32[]{:S(2)}) %collective-permute-start) | collective-permute-done | bytes 2097184 | tf_op jit(solution)/shard_map/ppermute | solution.py:13
  172.8 2.6 fusion.25
  176.1 41.7 %all-reduce.8.cloned.1.call-done = f32[128,128]{1,0:T(8,128)} async-done(((f32[128,128]{1,0:T(8,128)}), f32[128,128]{1,0:T(8,128)}) %all-reduce.8.cloned.1.call-update) | async-done | bytes 65552 | tf_op jit(solution)/shard_map/psum | solution.py:39
  217.8 1.2 fusion.115
  219.1 11.7 %cholesky.156 = f32[128,128]{1,0:T(8,128)S(1)} custom-call(f32[128,128]{1,0:T(8,128)S(1)} %fusion.66), custom_call_target="Cholesky" | custom-call | tf_op jit(solution)/shard_map/jit(cholesky)/cholesky | solution.py:28
  232.2 9.8 custom-call.14
  242.0 1.1 fusion.63
  243.1 1.1 fusion.116
  244.6 11.7 %cholesky.167 = f32[128,128]{1,0:T(8,128)S(1)} custom-call(f32[128,128]{1,0:T(8,128)S(1)} %fusion.62), custom_call_target="Cholesky" | custom-call | tf_op jit(solution)/shard_map/jit(cholesky)/cholesky | solution.py:28
  257.7 9.9 custom-call.15
  267.9 3.8 fusion.24
  271.8 2.1 fusion
  274.8 3.2 collective-permute-start.1
  278.0 52.6 %collective-permute-done.1 = f32[4096,128]{0,1:T(8,128)S(1)} collective-permute-done((f32[4096,128]{0,1:T(8,128)S(1)}, f32[4096,128]{0,1:T(8,128)S(1)}, u32[]{:S(2)}, u32[]{:S(2)}) %collective-permute-start.1) | collective-permute-done | bytes 2097184 | tf_op jit(solution)/shard_map/ppermute | solution.py:13
  330.8 1.0 copy-done.2
  331.8 2.6 fusion.23
  335.5 41.2 %all-reduce.10.cloned.1.call-done = f32[128,128]{1,0:T(8,128)} async-done(((f32[128,128]{1,0:T(8,128)}), f32[128,128]{1,0:T(8,128)}) %all-reduce.10.cloned.1.call-update) | async-done | bytes 65552 | tf_op jit(solution)/shard_map/psum | solution.py:39
  376.7 1.2 fusion.118
  378.0 11.7 %cholesky.178 = f32[128,128]{1,0:T(8,128)S(1)} custom-call(f32[128,128]{1,0:T(8,128)S(1)} %fusion.58), custom_call_target="Cholesky" | custom-call | tf_op jit(solution)/shard_map/jit(cholesky)/cholesky | solution.py:28
  391.1 9.8 custom-call.16
  400.9 1.1 fusion.55
  402.0 1.1 fusion.119
  403.6 11.7 %cholesky.189 = f32[128,128]{1,0:T(8,128)S(1)} custom-call(f32[128,128]{1,0:T(8,128)S(1)} %fusion.54), custom_call_target="Cholesky" | custom-call | tf_op jit(solution)/shard_map/jit(cholesky)/cholesky | solution.py:28
  416.6 9.9 custom-call.17
  426.9 3.8 fusion.22
  430.7 2.1 fusion.6
  433.8 3.2 collective-permute-start.2
  437.0 52.6 %collective-permute-done.2 = f32[4096,128]{0,1:T(8,128)S(1)} collective-permute-done((f32[4096,128]{0,1:T(8,128)S(1)}, f32[4096,128]{0,1:T(8,128)S(1)}, u32[]{:S(2)}, u32[]{:S(2)}) %collective-permute-start.2) | collective-permute-done | bytes 2097184 | tf_op jit(solution)/shard_map/ppermute | solution.py:13
  489.8 1.0 copy-done.3
  490.7 2.6 fusion.21
  494.0 41.7 %all-reduce.12.cloned.1.call-done = f32[128,128]{1,0:T(8,128)} async-done(((f32[128,128]{1,0:T(8,128)}), f32[128,128]{1,0:T(8,128)}) %all-reduce.12.cloned.1.call-update) | async-done | bytes 65552 | tf_op jit(solution)/shard_map/psum | solution.py:39
  535.7 1.2 fusion.121
  537.0 11.7 %cholesky.200 = f32[128,128]{1,0:T(8,128)S(1)} custom-call(f32[128,128]{1,0:T(8,128)S(1)} %fusion.50), custom_call_target="Cholesky" | custom-call | tf_op jit(solution)/shard_map/jit(cholesky)/cholesky | solution.py:28
  550.0 9.8 custom-call.18
  559.8 1.1 fusion.47
  561.0 1.1 fusion.122
  562.5 11.9 %cholesky.211 = f32[128,128]{1,0:T(8,128)S(1)} custom-call(f32[128,128]{1,0:T(8,128)S(1)} %fusion.46), custom_call_target="Cholesky" | custom-call | tf_op jit(solution)/shard_map/jit(cholesky)/cholesky | solution.py:28
  575.7 9.8 custom-call.19
  585.8 3.8 fusion.20
  589.7 2.1 fusion.12
  591.8 1.3 broadcast_select_fusion
  593.7 3.2 collective-permute-start.3
  597.6 0.7 fusion.88
  598.3 0.7 fusion.90
  599.6 339.6 %all-reduce = (f32[]{:T(128)}, f32[]{:T(128)}, f32[]{:T(128)}, f32[]{:T(128)}, f32[]{:T(128)}, /*index=5*/f32[]{:T(128)}, f32[]{:T(128)}, f32[]{:T(128)}) all-reduce(f32[]{:T(128)} %get-tuple-element.15, f32[]{:T(128)} %get-tuple-element.14, f32[]{:T(128)} %get-tuple-element.13, ...), channel_id=1, replica_groups=mesh['pair'=128,'row'=4] {'pair'}, use_global_device_ids=true, to_apply=%region_21.24 | all-reduce | flops 8 | bytes 64 | tf_op jit(solution)/shard_map/psum | solution.py:54
  945.0 2.7 fusion.102
  947.9 1.8 copy.14
  949.7 2.5 fusion.19
  952.2 59.3 %psum.95 = f32[128]{0:T(128)S(1)} all-reduce(f32[128]{0:T(128)S(1)} %fusion.19), channel_id=1, replica_groups=mesh['pair'=128,'row'=4] {'row'}, use_global_device_ids=true, to_apply=%region_7.10 | all-reduce | flops 128 | bytes 1024 | tf_op jit(solution)/shard_map/psum | solution.py:83
  (93 shorter events, 20.2 us)
Async XLA Ops:
  7.2 1.2 copy-start
  7.2 2.4 copy-start.10
  7.2 56.4 %all-reduce.6.cloned.1.call-start = ((), (), s32[]{:S(2)}) async-start(), calls=%async_computation | async-start | bytes 131072 | tf_op jit(solution)/shard_map/psum | solution.py:39
  9.5 208.3 %all-reduce.8.cloned.1.call-start = ((), (), s32[]{:S(2)}) async-start(), calls=%async_computation.1 | async-start | bytes 131072 | tf_op jit(solution)/shard_map/psum | solution.py:39
  90.0 24.9 %copy-start.9 = (bf16[4096,128]{1,0:T(8,128)(2,1)S(1)}, bf16[4096,128]{1,0:T(8,128)(2,1)}, u32[]{:S(2)}) copy-start(bf16[4096,128]{1,0:T(8,128)(2,1)} %param.7) | copy-start | bytes 3145732
  116.5 56.3 %copy-start.4 = (f32[4096,64]{0,1:T(8,128)}, f32[4096,64]{0,1:T(8,128)S(1)}, u32[]{:S(2)}) copy-start(f32[4096,64]{0,1:T(8,128)S(1)} %get-tuple-element.61) | copy-start | bytes 3145732
  116.8 55.8 %collective-permute-start = (f32[4096,128]{0,1:T(8,128)S(1)}, f32[4096,128]{0,1:T(8,128)S(1)}, u32[]{:S(2)}, u32[]{:S(2)}) collective-permute-start(f32[4096,128]{0,1:T(8,128)S(1)} %maximum_select_fusion), channel_id=1, source_target_pairs={{0,4},{4,8},{8,12},{12,16},{16,20},{20,24},{24,28},{28,32},{32,36}... | collective-permute-start | bytes 6291464 | tf_op jit(solution)/shard_map/ppermute | solution.py:13
  175.5 201.2 %all-reduce.10.cloned.1.call-start = ((), (), s32[]{:S(2)}) async-start(), calls=%async_computation.2 | async-start | bytes 131072 | tf_op jit(solution)/shard_map/psum | solution.py:39
  274.8 55.8 %collective-permute-start.1 = (f32[4096,128]{0,1:T(8,128)S(1)}, f32[4096,128]{0,1:T(8,128)S(1)}, u32[]{:S(2)}, u32[]{:S(2)}) collective-permute-start(f32[4096,128]{0,1:T(8,128)S(1)} %maximum_select_fusion.4), channel_id=1, source_target_pairs={{0,4},{4,8},{8,12},{12,16},{16,20},{20,24},{24,28},{28,32},{32,36}... | collective-permute-start | bytes 6291464 | tf_op jit(solution)/shard_map/ppermute | solution.py:13
  330.8 1.0 copy-start.2
  334.4 201.2 %all-reduce.12.cloned.1.call-start = ((), (), s32[]{:S(2)}) async-start(), calls=%async_computation.3 | async-start | bytes 131072 | tf_op jit(solution)/shard_map/psum | solution.py:39
  433.8 55.8 %collective-permute-start.2 = (f32[4096,128]{0,1:T(8,128)S(1)}, f32[4096,128]{0,1:T(8,128)S(1)}, u32[]{:S(2)}, u32[]{:S(2)}) collective-permute-start(f32[4096,128]{0,1:T(8,128)S(1)} %maximum_select_fusion.8), channel_id=1, source_target_pairs={{0,4},{4,8},{8,12},{12,16},{16,20},{20,24},{24,28},{28,32},{32,36}... | collective-permute-start | bytes 6291464 | tf_op jit(solution)/shard_map/ppermute | solution.py:13
  489.8 1.0 copy-start.3
  593.4 3.5 copy-start.5
  593.5 4.1 copy-start.6
  593.5 4.8 copy-start.7
  593.5 5.5 copy-start.8
  593.7 351.2 %collective-permute-start.3 = (f32[4096,128]{0,1:T(8,128)S(1)}, f32[4096,128]{0,1:T(8,128)}, u32[]{:S(2)}, u32[]{:S(2)}) collective-permute-start(f32[4096,128]{0,1:T(8,128)S(1)} %maximum_select_fusion.12), channel_id=1, source_target_pairs={{0,4},{4,8},{8,12},{12,16},{16,20},{20,24},{24,28},{28,32},{32,36}... | collective-permute-start | bytes 6291464 | tf_op jit(solution)/shard_map/ppermute | solution.py:13
  947.9 64.2 %copy-start.1 = (bf16[4096,128]{1,0:T(8,128)(2,1)S(1)}, bf16[4096,128]{1,0:T(8,128)(2,1)}, u32[]{:S(2)}) copy-start(bf16[4096,128]{1,0:T(8,128)(2,1)} %param.6) | copy-start | bytes 3145732
Sparse Core Ops, SparseCore 0:
  11.5 52.0 all-reduce.5
  175.6 42.1 all-reduce.7
  334.5 42.1 all-reduce.9
  493.5 42.1 all-reduce.11
where the time goes:
time: 1030 us; the launch traced here: 1020 us
  blocking collectives  399 us (39%)
  waiting for transfers between devices  335 us (33%)
  other arithmetic  194 us (19%)
  matrix products  44.6 us (4%)
  between operations  22.5 us (2%)
  starting transfers between devices  13.4 us (1%)
    psum x1, blocking collectives, on_device(): off_total, diag_total = lax.psum((off_part, diag_part), 'pair')  340 us
    psum x4, waiting for transfers between devices, full_gram(): return lax.psum(inner_product(factor, factor), 'row')  177 us
    ppermute x4, waiting for transfers between devices, from_behind(): return lax.ppermute(value, axis, pairs)  158 us
    another operation x24, other arithmetic, orthonormal(): lower = jnp.linalg.cholesky(square)  99.3 us
    another operation x16, other arithmetic, orthonormal(): return jax.scipy.linalg.solve_triangular(lower, block.T, lower=True).T  84.3 us
    psum x1, blocking collectives, on_device(): column_sq = lax.psum(jnp.sum(factor * factor, axis=0), 'row')  59.3 us
    dot_general x12, matrix products, product(): jnp.dot(left, right, precision=HIGH, preferred_element_type=jnp.float32)  24.2 us
  transfers between devices with their start and end apart: 8, of which 7 were waited for; matrix products, arithmetic and copies ran while one was open for 0% of the time, Pallas kernels for 0%

commit v1 on v0

--- a/solution.py
+++ b/solution.py
@@ -36,7 +36,7 @@
 
 
 def full_gram(factor):
-    return lax.psum(inner_product(factor, factor), "row")
+    return jnp.sum(lax.all_gather(inner_product(factor, factor), "row"), axis=0)
 
 
 def on_device(statistic, initial_basis, moving_slot):

time: 1030 us -> 859 us (0.83)
  waiting for transfers between devices: 335 us -> 158 us
  blocking collectives: 399 us -> 431 us
  matrix products: 44.6 us -> 31.3 us
  between operations: 22.5 us -> 9.37 us
    psum x4 -> x0, waiting for transfers between devices: 177 us -> none  [full_gram(): return lax.psum(inner_product(factor, factor), 'row')]
    all_gather x0 -> x4, blocking collectives: none -> 33.4 us  [full_gram(): return jnp.sum(lax.all_gather(inner_product(factor, factor), 'row'), axis=0)]
  transfers between devices with their start and end apart: 8 -> 4, of which waited for: 7 -> 3; matrix products, arithmetic and copies ran while one was open for 0% -> 0% of each run, Pallas kernels for 0% -> 0%
where the time goes in v1:
time: 859 us; the launch traced here: 849 us
  blocking collectives  431 us (50%)
  other arithmetic  203 us (24%)
  waiting for transfers between devices  158 us (18%)
  matrix products  31.3 us (4%)
  between operations  9.37 us (1%)
    psum x1, blocking collectives, on_device(): off_total, diag_total = lax.psum((off_part, diag_part), 'pair')  337 us
    ppermute x4, waiting for transfers between devices, from_behind(): return lax.ppermute(value, axis, pairs)  158 us
    another operation x24, other arithmetic, orthonormal(): lower = jnp.linalg.cholesky(square)  102 us
    another operation x16, other arithmetic, orthonormal(): return jax.scipy.linalg.solve_triangular(lower, block.T, lower=True).T  86 us
    psum x1, blocking collectives, on_device(): column_sq = lax.psum(jnp.sum(factor * factor, axis=0), 'row')  60.1 us
    all_gather x4, blocking collectives, full_gram(): return jnp.sum(lax.all_gather(inner_product(factor, factor), 'row'), axis=0)  33.4 us
    dot_general x12, matrix products, product(): jnp.dot(left, right, precision=HIGH, preferred_element_type=jnp.float32)  20.3 us
  transfers between devices with their start and end apart: 4, of which 3 were waited for; matrix products, arithmetic and copies ran while one was open for 0% of the time, Pallas kernels for 0%

profile of v1, /device:TPU:1, one launch (start us, length us, event | category | flops | bytes accessed | tf_op | source)
XLA Modules:
  0.0 848.9 jit_solution(10887585475683206478)
XLA Ops:
  0.6 1.5 fusion.110
  2.6 12.5 %all-gather = f32[512,128]{1,0:T(8,128)S(1)} all-gather(f32[128,128]{1,0:T(8,128)S(1)} %fusion.111), channel_id=2, replica_groups=mesh['pair'=128,'row'=4] {'row'}, dimensions={0}, use_global_device_ids=true | all-gather | bytes 327680 | tf_op jit(solution)/shard_map/all_gather | solution.py:39
  15.5 11.7 %cholesky.134 = f32[128,128]{1,0:T(8,128)S(1)} custom-call(f32[128,128]{1,0:T(8,128)S(1)} %fusion.74), custom_call_target="Cholesky" | custom-call | tf_op jit(solution)/shard_map/jit(cholesky)/cholesky | solution.py:28
  27.3 0.6 compare_reduce_fusion.7
  27.9 0.7 fusion.35
  28.6 9.8 %custom-call.12 = f32[1,128,128]{1,2,0:T(8,128)S(1)} custom-call(f32[1,128,128]{2,1,0:T(8,128)S(1)} %fusion.35), custom_call_target="InvertDiagBlocksLowerTriangular" | custom-call | tf_op jit(solution)/shard_map/jit(_solve_triangular)/triangular_solve | solution.py:29
  39.4 11.7 %cholesky.145 = f32[128,128]{1,0:T(8,128)S(1)} custom-call(f32[128,128]{1,0:T(8,128)S(1)} %fusion.70), custom_call_target="Cholesky" | custom-call | tf_op jit(solution)/shard_map/jit(cholesky)/cholesky | solution.py:28
  51.1 0.6 compare_reduce_fusion.6
  51.8 0.7 fusion.36
  52.4 10.0 %custom-call.13 = f32[1,128,128]{1,2,0:T(8,128)S(1)} custom-call(f32[1,128,128]{2,1,0:T(8,128)S(1)} %fusion.36), custom_call_target="InvertDiagBlocksLowerTriangular" | custom-call | tf_op jit(solution)/shard_map/jit(_solve_triangular)/triangular_solve | solution.py:29
  62.7 1.0 convolution_bitcast_fusion.1
  63.7 1.0 convolution_bitcast_fusion
  66.3 1.9 collective-permute-start
  68.9 54.0 %collective-permute-done = f32[4096,128]{0,1:T(8,128)S(1)} collective-permute-done((f32[4096,128]{0,1:T(8,128)S(1)}, f32[4096,128]{0,1:T(8,128)S(1)}, u32[]{:S(2)}, u32[]{:S(2)}) %collective-permute-start) | collective-permute-done | bytes 2097184 | tf_op jit(solution)/shard_map/ppermute | solution.py:13
  123.0 2.0 fusion.25
  125.1 6.3 all-gather.1
  131.8 11.7 %cholesky.156 = f32[128,128]{1,0:T(8,128)S(1)} custom-call(f32[128,128]{1,0:T(8,128)S(1)} %fusion.66), custom_call_target="Cholesky" | custom-call | tf_op jit(solution)/shard_map/jit(cholesky)/cholesky | solution.py:28
  143.5 0.6 compare_reduce_fusion.5
  144.2 0.7 fusion.37
  144.8 9.8 %custom-call.14 = f32[1,128,128]{1,2,0:T(8,128)S(1)} custom-call(f32[1,128,128]{2,1,0:T(8,128)S(1)} %fusion.37), custom_call_target="InvertDiagBlocksLowerTriangular" | custom-call | tf_op jit(solution)/shard_map/jit(_solve_triangular)/triangular_solve | solution.py:29
  155.6 11.7 %cholesky.167 = f32[128,128]{1,0:T(8,128)S(1)} custom-call(f32[128,128]{1,0:T(8,128)S(1)} %fusion.62), custom_call_target="Cholesky" | custom-call | tf_op jit(solution)/shard_map/jit(cholesky)/cholesky | solution.py:28
  167.4 0.6 compare_reduce_fusion.4
  168.0 0.7 fusion.38
  168.7 10.2 %custom-call.15 = f32[1,128,128]{1,2,0:T(8,128)S(1)} custom-call(f32[1,128,128]{2,1,0:T(8,128)S(1)} %fusion.38), custom_call_target="InvertDiagBlocksLowerTriangular" | custom-call | tf_op jit(solution)/shard_map/jit(_solve_triangular)/triangular_solve | solution.py:29
  179.1 3.7 fusion.24
  182.8 2.1 fusion
  185.9 1.9 collective-permute-start.1
  188.5 52.1 %collective-permute-done.1 = f32[4096,128]{0,1:T(8,128)S(1)} collective-permute-done((f32[4096,128]{0,1:T(8,128)S(1)}, f32[4096,128]{0,1:T(8,128)S(1)}, u32[]{:S(2)}, u32[]{:S(2)}) %collective-permute-start.1) | collective-permute-done | bytes 2097184 | tf_op jit(solution)/shard_map/ppermute | solution.py:13
  240.8 2.0 fusion.23
  242.8 7.2 all-gather.2
  250.0 1.0 reduce_sum.119
  251.4 11.7 %cholesky.178 = f32[128,128]{1,0:T(8,128)S(1)} custom-call(f32[128,128]{1,0:T(8,128)S(1)} %fusion.58), custom_call_target="Cholesky" | custom-call | tf_op jit(solution)/shard_map/jit(cholesky)/cholesky | solution.py:28
  263.7 0.7 fusion.39
  264.4 9.8 %custom-call.16 = f32[1,128,128]{1,2,0:T(8,128)S(1)} custom-call(f32[1,128,128]{2,1,0:T(8,128)S(1)} %fusion.39), custom_call_target="InvertDiagBlocksLowerTriangular" | custom-call | tf_op jit(solution)/shard_map/jit(_solve_triangular)/triangular_solve | solution.py:29
  275.8 12.5 %cholesky.189 = f32[128,128]{1,0:T(8,128)S(1)} custom-call(f32[128,128]{1,0:T(8,128)} %fusion.54), custom_call_target="Cholesky" | custom-call | tf_op jit(solution)/shard_map/jit(cholesky)/cholesky | solution.py:28
  289.0 0.7 fusion.40
  289.7 10.0 %custom-call.17 = f32[1,128,128]{1,2,0:T(8,128)S(1)} custom-call(f32[1,128,128]{2,1,0:T(8,128)S(1)} %fusion.40), custom_call_target="InvertDiagBlocksLowerTriangular" | custom-call | tf_op jit(solution)/shard_map/jit(_solve_triangular)/triangular_solve | solution.py:29
  300.0 3.7 fusion.22
  303.7 2.1 fusion.6
  306.7 1.9 collective-permute-start.2
  309.3 52.1 %collective-permute-done.2 = f32[4096,128]{0,1:T(8,128)S(1)} collective-permute-done((f32[4096,128]{0,1:T(8,128)S(1)}, f32[4096,128]{0,1:T(8,128)S(1)}, u32[]{:S(2)}, u32[]{:S(2)}) %collective-permute-start.2) | collective-permute-done | bytes 2097184 | tf_op jit(solution)/shard_map/ppermute | solution.py:13
  361.6 2.0 fusion.21
  363.6 7.4 all-gather.3
  371.1 1.0 reduce_sum.120
  373.1 12.5 %cholesky.200 = f32[128,128]{1,0:T(8,128)S(1)} custom-call(f32[128,128]{1,0:T(8,128)} %fusion.50), custom_call_target="Cholesky" | custom-call | tf_op jit(solution)/shard_map/jit(cholesky)/cholesky | solution.py:28
  386.3 0.7 fusion.41
  387.0 9.8 %custom-call.18 = f32[1,128,128]{1,2,0:T(8,128)S(1)} custom-call(f32[1,128,128]{2,1,0:T(8,128)S(1)} %fusion.41), custom_call_target="InvertDiagBlocksLowerTriangular" | custom-call | tf_op jit(solution)/shard_map/jit(_solve_triangular)/triangular_solve | solution.py:29
  397.6 0.7 copy.22
  398.3 1.5 fusion.46
  399.8 12.5 %cholesky.211 = f32[128,128]{1,0:T(8,128)S(1)} custom-call(f32[128,128]{1,0:T(8,128)} %fusion.46), custom_call_target="Cholesky" | custom-call | tf_op jit(solution)/shard_map/jit(cholesky)/cholesky | solution.py:28
  413.0 1.3 fusion.42
  414.3 10.8 %custom-call.19 = f32[1,128,128]{1,2,0:T(8,128)S(1)} custom-call(f32[1,128,128]{2,1,0:T(8,128)} %fusion.42), custom_call_target="InvertDiagBlocksLowerTriangular" | custom-call | tf_op jit(solution)/shard_map/jit(_solve_triangular)/triangular_solve | solution.py:29
  425.4 3.6 fusion.20
  429.1 2.1 fusion.12
  431.2 1.3 broadcast_select_fusion
  433.1 1.9 collective-permute-start.3
  435.0 0.6 fusion.86
  435.7 0.7 fusion.88
  436.4 0.7 fusion.90
  437.7 337.5 %all-reduce = (f32[]{:T(128)}, f32[]{:T(128)}, f32[]{:T(128)}, f32[]{:T(128)}, f32[]{:T(128)}, /*index=5*/f32[]{:T(128)}, f32[]{:T(128)}, f32[]{:T(128)}) all-reduce(f32[]{:T(128)} %get-tuple-element.18, f32[]{:T(128)} %get-tuple-element.17, f32[]{:T(128)} %get-tuple-element.16, ...), channel_id=1, replica_groups=mesh['pair'=128,'row'=4] {'pair'}, use_global_device_ids=true, to_apply=%region_21.24 | all-reduce | flops 8 | bytes 64 | tf_op jit(solution)/shard_map/psum | solution.py:54
  781.0 2.7 fusion.102
  783.9 1.8 copy.23
  785.7 2.5 fusion.19
  788.1 60.1 %psum.63 = f32[128]{0:T(128)S(1)} all-reduce(f32[128]{0:T(128)S(1)} %fusion.19), channel_id=1, replica_groups=mesh['pair'=128,'row'=4] {'row'}, use_global_device_ids=true, to_apply=%region_7.10 | all-reduce | flops 128 | bytes 1024 | tf_op jit(solution)/shard_map/psum | solution.py:83
  (79 shorter events, 16.8 us)
Async XLA Ops:
  0.6 1.5 copy-start
  39.0 24.8 %copy-start.5 = (bf16[4096,128]{1,0:T(8,128)(2,1)S(1)}, bf16[4096,128]{1,0:T(8,128)(2,1)}, u32[]{:S(2)}) copy-start(bf16[4096,128]{1,0:T(8,128)(2,1)} %param.7) | copy-start | bytes 3145732
  66.0 57.1 %copy-start.4 = (f32[4096,64]{0,1:T(8,128)}, f32[4096,64]{0,1:T(8,128)S(1)}, u32[]{:S(2)}) copy-start(f32[4096,64]{0,1:T(8,128)S(1)} %get-tuple-element.64) | copy-start | bytes 3145732
  66.3 56.6 %collective-permute-start = (f32[4096,128]{0,1:T(8,128)S(1)}, f32[4096,128]{0,1:T(8,128)S(1)}, u32[]{:S(2)}, u32[]{:S(2)}) collective-permute-start(f32[4096,128]{0,1:T(8,128)S(1)} %maximum_select_fusion), channel_id=1, source_target_pairs={{0,4},{4,8},{8,12},{12,16},{16,20},{20,24},{24,28},{28,32},{32,36}... | collective-permute-start | bytes 6291464 | tf_op jit(solution)/shard_map/ppermute | solution.py:13
  185.9 54.7 %collective-permute-start.1 = (f32[4096,128]{0,1:T(8,128)S(1)}, f32[4096,128]{0,1:T(8,128)S(1)}, u32[]{:S(2)}, u32[]{:S(2)}) collective-permute-start(f32[4096,128]{0,1:T(8,128)S(1)} %maximum_select_fusion.4), channel_id=1, source_target_pairs={{0,4},{4,8},{8,12},{12,16},{16,20},{20,24},{24,28},{28,32},{32,36}... | collective-permute-start | bytes 6291464 | tf_op jit(solution)/shard_map/ppermute | solution.py:13
  240.8 2.0 copy-start.3
  306.7 54.7 %collective-permute-start.2 = (f32[4096,128]{0,1:T(8,128)S(1)}, f32[4096,128]{0,1:T(8,128)S(1)}, u32[]{:S(2)}, u32[]{:S(2)}) collective-permute-start(f32[4096,128]{0,1:T(8,128)S(1)} %maximum_select_fusion.8), channel_id=1, source_target_pairs={{0,4},{4,8},{8,12},{12,16},{16,20},{20,24},{24,28},{28,32},{32,36}... | collective-permute-start | bytes 6291464 | tf_op jit(solution)/shard_map/ppermute | solution.py:13
  361.6 2.0 copy-start.2
  433.1 347.9 %collective-permute-start.3 = (f32[4096,128]{0,1:T(8,128)S(1)}, f32[4096,128]{0,1:T(8,128)}, u32[]{:S(2)}, u32[]{:S(2)}) collective-permute-start(f32[4096,128]{0,1:T(8,128)S(1)} %maximum_select_fusion.12), channel_id=1, source_target_pairs={{0,4},{4,8},{8,12},{12,16},{16,20},{20,24},{24,28},{28,32},{32,36}... | collective-permute-start | bytes 6291464 | tf_op jit(solution)/shard_map/ppermute | solution.py:13
  783.8 64.9 %copy-start.1 = (bf16[4096,128]{1,0:T(8,128)(2,1)S(1)}, bf16[4096,128]{1,0:T(8,128)(2,1)}, u32[]{:S(2)}) copy-start(bf16[4096,128]{1,0:T(8,128)(2,1)} %param.6) | copy-start | bytes 3145732
